TPU v7x, 32 devices: a whole 2x2x4 slice. The times are simulated.
32 devices in a mesh: dp: 8 (over y, x, core), tensor: 4 (over z).
Axes of the slice: x: 2, y: 2, z: 4, core: 2. Of those that a mesh axis runs over, the one named last changes fastest.
Arguments:
- inputs: bfloat16 [24, 1024, 768], P('dp', 'tensor'), may hold values from -6 to 6
- cotangent: bfloat16 [24, 1024, 768], P('dp', 'tensor'), may hold values from -6 to 6
- w_qkv: bfloat16 [768, 3, 768], P('dp', None, 'tensor'), may hold values from -0.21875 to 0.21875
- b_qkv: bfloat16 [3, 768], P(None, 'dp'), may hold values from -3 to 3
- w_attn_out: bfloat16 [768, 768], P('tensor', 'dp'), may hold values from -1.75 to 1.75
- w_up: bfloat16 [768, 3072], P('dp', 'tensor'), may hold values from -0.21875 to 0.21875
- b_up: bfloat16 [3072], P('dp'), may hold values from -3 to 3
- w_down: bfloat16 [3072, 768], P('tensor', 'dp'), may hold values from -0.109375 to 0.109375
- vectors: bfloat16 [5, 768], P(None, 'dp'), may hold values from 0.25 to 1.75
Outputs:
- output: bfloat16 [24, 1024, 768], P('dp', 'tensor')
- grad_inputs: bfloat16 [24, 1024, 768], P('dp', 'tensor')
- grad_w_qkv: float32 [768, 3, 768], P('dp', None, 'tensor')
- grad_b_qkv: float32 [3, 768], P(None, 'dp')
- grad_w_attn_out: float32 [768, 768], P('tensor', 'dp')
- grad_w_up: float32 [768, 3072], P('dp', 'tensor')
- grad_b_up: float32 [3072], P('dp')
- grad_w_down: float32 [3072, 768], P('tensor', 'dp')
- grad_vectors: float32 [5, 768], P(None, 'dp')
All inputs are finite; a program needn't handle non-finite values.
Results may differ from a plain program's by a relative error of at most 0.012.
The roundings to bfloat16 on the way count: a program that leaves them out, or rounds other values in their place, can miss the bound.
Values may be sent and summed in bfloat16 or wider, within the bound.
A program may use at most 128 MiB of HBM per device.

v0:
```python
import jax
import jax.numpy as jnp
from jax import lax
from jax.sharding import PartitionSpec as P

HD = 64
ROT = 16


EPSILON = 1e-05
NEGATIVE = -1e30


def rope_tables(length):
    halfwidth = ROT // 2
    positions = jnp.arange(length).astype(jnp.float32)
    frequency = 10000.0 ** (-jnp.arange(halfwidth).astype(jnp.float32) / halfwidth)
    angles = positions[:, None] * frequency[None, :]
    return (jnp.cos(angles)[:, None, :], jnp.sin(angles)[:, None, :])


def rotate(tensor, cosine, sines):
    halfwidth = ROT // 2
    lower_half = tensor[..., :halfwidth]
    upper_half = tensor[..., halfwidth:ROT]
    return jnp.concatenate(
        [
            lower_half * cosine - upper_half * sines,
            upper_half * cosine + lower_half * sines,
            tensor[..., ROT:],
        ],
        axis=-1,
    )


def unrotate(tensor, cosine, sines):
    halfwidth = ROT // 2
    lower_half = tensor[..., :halfwidth]
    upper_half = tensor[..., halfwidth:ROT]
    return jnp.concatenate(
        [
            lower_half * cosine + upper_half * sines,
            upper_half * cosine - lower_half * sines,
            tensor[..., ROT:],
        ],
        axis=-1,
    )


def normalize(values):
    centre = values - jnp.mean(values, -1, keepdims=True)
    rsigma = lax.rsqrt(jnp.mean(centre * centre, -1, keepdims=True) + EPSILON)
    return (centre * rsigma, rsigma)


def norm_backward(grad_normed, gain_row, normed, rsigma):
    scaled = grad_normed * gain_row
    return rsigma * (
        scaled
        - jnp.mean(scaled, -1, keepdims=True)
        - normed * jnp.mean(scaled * normed, -1, keepdims=True)
    )


def gelu_slope(values):
    cumulative = 0.5 * (1.0 + lax.erf(values * 0.7071067811865476))
    density = jnp.exp(-0.5 * values * values) * 0.3989422804014327
    return cumulative + values * density


def masked_scores(queries, keys_rot):
    length = queries.shape[0]
    scores = jnp.einsum(
        "qhe,khe->hqk", queries, keys_rot, preferred_element_type=jnp.float32
    ) * HD ** (-0.5)
    positions = jnp.arange(length)
    return jnp.where((positions[None, :] <= positions[:, None])[None], scores, NEGATIVE)


def attend(triple):
    queries, keys_rot, values_in = triple
    scores = masked_scores(queries, keys_rot)
    largest = jnp.max(scores, -1, keepdims=True)
    weights = jnp.exp(scores - largest)
    totals = jnp.sum(weights, -1, keepdims=True)
    weights = weights / totals
    attended = jnp.einsum(
        "hqk,khe->qhe", weights.astype(jnp.bfloat16), values_in, preferred_element_type=jnp.float32
    )
    return (attended.astype(jnp.bfloat16), (largest + jnp.log(totals))[..., 0])


def attend_back(bundle):
    queries, keys_rot, values_in, incoming_gradient, logsum = bundle
    scores = masked_scores(queries, keys_rot)
    weights = jnp.exp(scores - logsum[..., None])
    grad_values = jnp.einsum(
        "hqk,qhe->khe",
        weights.astype(jnp.bfloat16),
        incoming_gradient,
        preferred_element_type=jnp.float32,
    )
    grad_weights = jnp.einsum(
        "qhe,khe->hqk", incoming_gradient, values_in, preferred_element_type=jnp.float32
    )
    row_inner = jnp.sum(weights * grad_weights, -1, keepdims=True)
    grad_scores = (weights * (grad_weights - row_inner)).astype(jnp.bfloat16)
    score_scale = HD ** (-0.5)
    grad_queries = (
        jnp.einsum("hqk,khe->qhe", grad_scores, keys_rot, preferred_element_type=jnp.float32)
        * score_scale
    )
    grad_keys = (
        jnp.einsum("hqk,qhe->khe", grad_scores, queries, preferred_element_type=jnp.float32)
        * score_scale
    )
    return (grad_queries, grad_keys, grad_values)


def local(inputs, cotangent, w_qkv, b_qkv, w_attn_out, w_up, b_up, w_down, vectors):
    (
        complete_query_key_value,
        bias_qkv,
        complete_output_weight,
        complete_up_weight,
        bias_up,
        complete_down_weight,
        vector_rows,
    ) = (
        lax.all_gather(w_qkv, "dp", axis=0, tiled=True),
        lax.all_gather(b_qkv, "dp", axis=1, tiled=True),
        lax.all_gather(w_attn_out, "dp", axis=1, tiled=True),
        lax.all_gather(w_up, "dp", axis=0, tiled=True),
        lax.all_gather(b_up, "dp", axis=0, tiled=True),
        lax.all_gather(w_down, "dp", axis=1, tiled=True),
        lax.all_gather(vectors, "dp", axis=1, tiled=True),
    )
    row_values = vector_rows.astype(jnp.float32)
    tensor_pos = lax.axis_index("tensor")
    local_width = complete_query_key_value.shape[2]
    local_hidden = complete_up_weight.shape[1]
    heads_local = local_width // HD
    qkv_offset = lax.dynamic_slice_in_dim(
        bias_qkv, tensor_pos * local_width, local_width, 1
    ).astype(jnp.float32)
    up_offset = lax.dynamic_slice_in_dim(
        bias_up, tensor_pos * local_hidden, local_hidden, 0
    ).astype(jnp.float32)
    residual = inputs.astype(jnp.float32)
    normed_local, rsigma_local = normalize(residual)
    first_low = (normed_local * row_values[0] + row_values[1]).astype(jnp.bfloat16)
    second_low = (normed_local * row_values[2] + row_values[3]).astype(jnp.bfloat16)
    first_branch_input, second_branch_input = (
        lax.all_gather(first_low, "tensor", axis=1, tiled=True),
        lax.all_gather(second_low, "tensor", axis=1, tiled=True),
    )
    sequences = first_branch_input.shape[0]
    length = first_branch_input.shape[1]
    projected = (
        jnp.einsum(
            "vpk,knu->vpnu",
            first_branch_input,
            complete_query_key_value,
            preferred_element_type=jnp.float32,
        )
        + qkv_offset
    )
    projected = projected.reshape(sequences, length, 3, heads_local, HD)
    cosine, sines = rope_tables(length)
    queries = rotate(projected[:, :, 0], cosine, sines).astype(jnp.bfloat16)
    keys_rot = rotate(projected[:, :, 1], cosine, sines).astype(jnp.bfloat16)
    values_in = projected[:, :, 2].astype(jnp.bfloat16)
    attended, logsum = lax.map(attend, (queries, keys_rot, values_in))
    attention_rows_flat = attended.reshape(sequences, length, local_width)
    partial_value = jnp.einsum(
        "piw,wu->piu",
        attention_rows_flat,
        complete_output_weight,
        preferred_element_type=jnp.float32,
    )
    hidden_pre = (
        jnp.einsum(
            "kgm,mu->kgu",
            second_branch_input,
            complete_up_weight,
            preferred_element_type=jnp.float32,
        )
        + up_offset
    )
    gelu_hidden_output = jax.nn.gelu(hidden_pre, approximate=False).astype(jnp.bfloat16)
    partial_value = partial_value + jnp.einsum(
        "piw,wu->piu", gelu_hidden_output, complete_down_weight, preferred_element_type=jnp.float32
    )
    summed = lax.psum_scatter(partial_value, "tensor", scatter_dimension=1, tiled=True)
    output = (residual + summed + row_values[4]).astype(jnp.bfloat16)
    (
        complete_query_key_value,
        complete_output_weight,
        complete_up_weight,
        complete_down_weight,
        vector_rows,
    ) = (
        lax.all_gather(w_qkv, "dp", axis=0, tiled=True),
        lax.all_gather(w_attn_out, "dp", axis=1, tiled=True),
        lax.all_gather(w_up, "dp", axis=0, tiled=True),
        lax.all_gather(w_down, "dp", axis=1, tiled=True),
        lax.all_gather(vectors, "dp", axis=1, tiled=True),
    )
    row_values = vector_rows.astype(jnp.float32)
    incoming_gradient = lax.all_gather(cotangent, "tensor", axis=1, tiled=True)
    activation_gradient = jnp.einsum(
        "ibo,wo->ibw", incoming_gradient, complete_down_weight, preferred_element_type=jnp.float32
    )
    down_weight_gradient = jnp.einsum(
        "qea,qeh->ah", gelu_hidden_output, incoming_gradient, preferred_element_type=jnp.float32
    )
    preactivation_gradient = (activation_gradient * gelu_slope(hidden_pre)).astype(jnp.bfloat16)
    grad_bias_up = jnp.sum(preactivation_gradient, axis=(0, 1), dtype=jnp.float32)
    up_weight_gradient = jnp.einsum(
        "xvk,xvz->kz",
        second_branch_input,
        preactivation_gradient,
        preferred_element_type=jnp.float32,
    )
    second_branch_gradient = jnp.einsum(
        "rae,ne->ran",
        preactivation_gradient,
        complete_up_weight,
        preferred_element_type=jnp.float32,
    )
    grad_attended = jnp.einsum(
        "ibo,wo->ibw", incoming_gradient, complete_output_weight, preferred_element_type=jnp.float32
    ).astype(jnp.bfloat16)
    grad_out = jnp.einsum(
        "qea,qeh->ah", attention_rows_flat, incoming_gradient, preferred_element_type=jnp.float32
    )
    grad_query, grad_key, grad_value = lax.map(
        attend_back,
        (
            queries,
            keys_rot,
            values_in,
            grad_attended.reshape(sequences, length, heads_local, HD),
            logsum,
        ),
    )
    projection_gradient = jnp.stack(
        [unrotate(grad_query, cosine, sines), unrotate(grad_key, cosine, sines), grad_value], axis=2
    )
    projection_gradient = projection_gradient.reshape(sequences, length, 3, local_width).astype(
        jnp.bfloat16
    )
    grad_bias_qkv = jnp.sum(projection_gradient, axis=(0, 1), dtype=jnp.float32)
    query_key_value_gradient = jnp.einsum(
        "poa,pohn->ahn", first_branch_input, projection_gradient, preferred_element_type=jnp.float32
    )
    grad_first = jnp.einsum(
        "upvh,evh->upe",
        projection_gradient,
        complete_query_key_value,
        preferred_element_type=jnp.float32,
    )
    cot_local = cotangent.astype(jnp.float32)
    grad_norm_one, grad_norm_two = (
        lax.psum_scatter(grad_first, "tensor", scatter_dimension=1, tiled=True),
        lax.psum_scatter(second_branch_gradient, "tensor", scatter_dimension=1, tiled=True),
    )
    through_norms = norm_backward(
        grad_norm_one, row_values[0], normed_local, rsigma_local
    ) + norm_backward(grad_norm_two, row_values[2], normed_local, rsigma_local)
    grad_input = cot_local + through_norms
    vector_grads = jnp.stack(
        [
            jnp.sum(grad_norm_one * normed_local, axis=(0, 1)),
            jnp.sum(grad_norm_one, axis=(0, 1)),
            jnp.sum(grad_norm_two * normed_local, axis=(0, 1)),
            jnp.sum(grad_norm_two, axis=(0, 1)),
            jnp.sum(cot_local, axis=(0, 1)),
        ]
    )
    model_width = complete_query_key_value.shape[0]
    bias_qkv_full = lax.dynamic_update_slice_in_dim(
        jnp.zeros((3, model_width), jnp.float32), grad_bias_qkv, tensor_pos * local_width, 1
    )
    bias_up_full = lax.dynamic_update_slice_in_dim(
        jnp.zeros((local_hidden * lax.axis_size("tensor"),), jnp.float32),
        grad_bias_up,
        tensor_pos * local_hidden,
        0,
    )
    shares = (
        lax.psum_scatter(query_key_value_gradient, "dp", scatter_dimension=0, tiled=True),
        lax.psum_scatter(grad_out, "dp", scatter_dimension=1, tiled=True),
        lax.psum_scatter(up_weight_gradient, "dp", scatter_dimension=0, tiled=True),
        lax.psum_scatter(down_weight_gradient, "dp", scatter_dimension=1, tiled=True),
        lax.psum_scatter(bias_qkv_full, "dp", scatter_dimension=1, tiled=True),
        lax.psum_scatter(bias_up_full, "dp", scatter_dimension=0, tiled=True),
        lax.psum_scatter(vector_grads, "dp", scatter_dimension=1, tiled=True),
    )
    reduced = lax.psum((shares[4], shares[5], shares[6]), "tensor")
    return (
        output,
        grad_input.astype(jnp.bfloat16),
        shares[0],
        reduced[0],
        shares[1],
        shares[2],
        reduced[1],
        shares[3],
        reduced[2],
    )


def solution(mesh):
    placed = (
        P("dp", "tensor", None),
        P("dp", "tensor", None),
        P("dp", None, "tensor"),
        P(None, "dp"),
        P("tensor", "dp"),
        P("dp", "tensor"),
        P("dp"),
        P("tensor", "dp"),
        P(None, "dp"),
    )
    return jax.shard_map(
        local,
        mesh=mesh,
        in_specs=placed,
        out_specs=(
            P("dp", "tensor", None),
            P("dp", "tensor", None),
            P("dp", None, "tensor"),
            P(None, "dp"),
            P("tensor", "dp"),
            P("dp", "tensor"),
            P("dp"),
            P("tensor", "dp"),
            P(None, "dp"),
        ),
        check_vma=False,
    )
```

profile of v0, /device:TPU:0, one launch (start us, length us, event | category | flops | bytes accessed | tf_op | source)
XLA Modules:
  0.0 1095.5 jit_solution(848721837684816109)
XLA Ops:
  7.2 10.5 all-gather
  28.1 13.2 %all_gather.37 = bf16[768,3,192]{2,1,0:T(4,128)(2,1)S(1)} all-gather(bf16[96,3,192]{2,1,0:T(4,128)(2,1)S(1)} %copy.70), channel_id=1, replica_groups=mesh['dp'=8,'tensor'=4] {'dp'}, dimensions={0}, use_global_device_ids=true | all-gather | bytes 995328 | tf_op jit(solution)/shard_map/all_gather | solution.py:130
  50.5 10.6 all_gather.39
  61.4 53.7 %all-gather.9.cloned.1.call-done = bf16[3,1024,768]{2,1,0:T(8,128)(2,1)} async-done(((bf16[3,256,768]{2,1,0:T(8,128)(2,1)}), bf16[3,1024,768]{2,1,0:T(8,128)(2,1)}) %all-gather.9.cloned.1.call-update) | async-done | bytes 4718608 | tf_op jit(solution)/shard_map/all_gather | solution.py:154
  125.3 44.3 %while.26 = (s32[]{:T(128)}, bf16[3,1024,3,64]{1,3,2,0:T(8,128)(2,1)}, f32[3,3,1024]{2,1,0:T(4,128)}, bf16[3,1024,3,64]{1,3,2,0:T(8,128)(2,1)}, bf16[3,1024,3,64...) while((s32[]{:T(128)}, bf16[3,1024,3,64]{1,3,2,0:T(8,128)(2,1)}, ...), condition=%wide.region_5.6_spmd, body=%wide.region_2.5_spmd.sunk | while | flops 844297216 | bytes 47814772 | solution.py:173
  169.6 34.9 %all-gather.17.cloned.1.call-done = bf16[3,1024,768]{2,1,0:T(8,128)(2,1)} async-done(((bf16[3,256,768]{2,1,0:T(8,128)(2,1)}), bf16[3,1024,768]{2,1,0:T(8,128)(2,1)}) %all-gather.17.cloned.1.call-update) | async-done | bytes 4718608 | tf_op jit(solution)/shard_map/all_gather | solution.py:210
  208.6 82.7 %while.27 = (s32[]{:T(128)}, f32[3,1024,3,64]{1,3,2,0:T(8,128)}, f32[3,1024,3,64]{1,3,2,0:T(8,128)}, bf16[3,1024,3,64]{1,3,2,0:T(8,128)(2,1)}, bf16[3,1024,3,64]...) while((s32[]{:T(128)}, f32[3,1024,3,64]{1,3,2,0:T(8,128)}, ...), condition=%wide.region_9.10_spmd, body=%wide.region_7.9_spmd.sunk | while | flops 2061890560 | bytes 103777392 | solution.py:237
  303.6 9.3 all-gather.2
  319.9 13.8 %fusion.102 = (u8[1024,768]{1,0:T(8,128)(4,1)S(1)}, u8[1024,768]{1,0:T(8,128)(4,1)}, f32[3,1024,768]{2,1,0:T(8,128)}) fusion(f32[768]{0:T(1024)S(1)} %dynamic-slice_convert_fusion, bf16[3,1024,768]{2,1,0:T(8,128)(2,1)} %all-gather.11.cloned.1.call-done, bf16[768,768]{1,0:T(8,128)(2,1)} %all-gather.13.cloned.1.call-done), kind=kOutput, calls=%fused_computation.135 | convolution fusion | flops 3655335936 | bytes 16911360 | tf_op jit(solution)/shard_map/kgm,mu->kgu/dot_general | solution.py:182
  333.7 10.5 all-gather.15.cloned.1.call-done
  344.1 10.4 convert_reduce_fusion
  363.2 23.4 %fusion.56 = bf16[3,1024,768]{2,1,0:T(8,128)(2,1)S(1)} fusion(f32[3,1024,768]{2,1,0:T(8,128)} %get-tuple-element.173, f32[768]{0:T(1024)S(1)} %dynamic-slice_convert_fusion, u8[1024,768]{1,0:T(8,128)(4,1)} %get-tuple-element.97, u8[1024,768]{1,0:T(8,128)(4,1)S(1)} %get-tuple-element.96), kind=kLoop, calls=%fused_computation.65 | loop fusion | flops 167510016 | bytes 15731712 | tf_op jit(solution)/shard_map/convert_element_type | solution.py:190
  404.3 103.4 %reduce-scatter.18.cloned.1.call-done = f32[3,256,768]{2,1,0:T(8,128)} async-done(((f32[3,1024,768]{2,1,0:T(8,128)}), f32[3,256,768]{2,1,0:T(8,128)}) %reduce-scatter.18.cloned.1.call-update) | async-done | bytes 2359312 | tf_op jit(solution)/shard_map/reduce_scatter | solution.py:265
  507.7 164.5 %reduce-scatter.20.cloned.1.call-done = f32[3,256,768]{2,1,0:T(8,128)} async-done(((f32[3,1024,768]{2,1,0:T(8,128)}), f32[3,256,768]{2,1,0:T(8,128)}) %reduce-scatter.20.cloned.1.call-update) | async-done | bytes 2359312 | tf_op jit(solution)/shard_map/reduce_scatter | solution.py:266
  680.5 156.2 %reduce-scatter.16.cloned.1.call-done = f32[3,256,768]{2,1,0:T(8,128)} async-done(((f32[3,1024,768]{2,1,0:T(8,128)}), f32[3,256,768]{2,1,0:T(8,128)}) %reduce-scatter.16.cloned.1.call-update) | async-done | bytes 2359312 | tf_op jit(solution)/shard_map/reduce_scatter | solution.py:194
  852.1 9.1 convolution_bitcast_fusion.2
  861.3 9.1 convolution_bitcast_fusion.1
  871.9 23.6 %all-reduce = f32[3072]{0:T(1024)S(1)} all-reduce(f32[3072]{0:T(1024)S(1)} %dynamic_update_slice.25), channel_id=9, replica_groups=mesh['dp'=8,'tensor'=4] {'dp'}, use_global_device_ids=true, to_apply=%region_23.24.clone | all-reduce | flops 3072 | bytes 24576
  896.5 16.0 %reduce-scatter.30.cloned.1.call-done = f32[96,192]{1,0:T(8,128)} async-done(((f32[768,192]{1,0:T(8,128)}), f32[96,192]{1,0:T(8,128)}) %reduce-scatter.30.cloned.1.call-update) | async-done | bytes 73744
  914.1 35.3 %reduce-scatter.32.cloned.1.call-done = f32[96,5]{1,0:T(8,128)} async-done(((f32[768,5]{1,0:T(8,128)}), f32[96,5]{1,0:T(8,128)}) %reduce-scatter.32.cloned.1.call-update) | async-done | bytes 1936
  950.3 12.4 %all-reduce.1 = (f32[3,96]{1,0:T(4,128)}, f32[384]{0:T(512)}, f32[5,96]{1,0:T(8,128)}) all-reduce(f32[3,96]{1,0:T(4,128)S(1)} %copy.100, f32[384]{0:T(512)S(1)} %dynamic-slice.2, f32[5,96]{1,0:T(8,128)S(1)} %copy.104), channel_id=1, replica_groups=mesh['dp'=8,'tensor'=4] {'tensor'}, use_global_device_ids=true, to_apply=%region_19.20 | all-reduce | flops 1152 | bytes 9216 | tf_op jit(solution)/shard_map/psum | solution.py:300
  962.7 33.0 %reduce-scatter.22.cloned.1.call-done = f32[96,3,192]{2,0,1:T(8,128)} async-done(((f32[768,3,192]{2,0,1:T(8,128)}), f32[96,3,192]{2,0,1:T(8,128)}) %reduce-scatter.22.cloned.1.call-update) | async-done | bytes 221200 | tf_op jit(solution)/shard_map/reduce_scatter | solution.py:292
  995.7 46.8 %reduce-scatter.24.cloned.1.call-done = f32[96,768]{1,0:T(8,128)} async-done(((f32[768,768]{1,0:T(8,128)}), f32[96,768]{1,0:T(8,128)}) %reduce-scatter.24.cloned.1.call-update) | async-done | bytes 294928 | tf_op jit(solution)/shard_map/reduce_scatter | solution.py:294
  1042.5 46.3 %reduce-scatter.26.cloned.1.call-done = f32[768,96]{0,1:T(8,128)} async-done(((f32[768,768]{0,1:T(8,128)}), f32[768,96]{0,1:T(8,128)}) %reduce-scatter.26.cloned.1.call-update) | async-done | bytes 294928 | tf_op jit(solution)/shard_map/reduce_scatter | solution.py:295
  (210 shorter events, 234.0 us)
Async XLA Ops:
  7.2 107.9 %all-gather.9.cloned.1.call-start = ((), (), s32[]{:S(2)}) async-start(), calls=%async_computation.9 | async-start | bytes 5898240 | tf_op jit(solution)/shard_map/all_gather | solution.py:154
  25.2 179.3 %all-gather.17.cloned.1.call-start = ((), (), s32[]{:S(2)}) async-start(), calls=%async_computation.14 | async-start | bytes 5898240 | tf_op jit(solution)/shard_map/all_gather | solution.py:210
  26.0 287.1 %all-gather.13.cloned.1.call-start = ((), (), s32[]{:S(2)}) async-start(), calls=%async_computation.11 | async-start | bytes 1327104 | tf_op jit(solution)/shard_map/all_gather | solution.py:133
  26.7 293.2 %all-gather.11.cloned.1.call-start = ((), (), s32[]{:S(2)}) async-start(), calls=%async_computation.10 | async-start | bytes 5898240 | tf_op jit(solution)/shard_map/all_gather | solution.py:155
  27.3 316.9 %all-gather.15.cloned.1.call-start = ((), (), s32[]{:S(2)}) async-start(), calls=%async_computation.12 | async-start | bytes 1327104 | tf_op jit(solution)/shard_map/all_gather | solution.py:135
  27.9 479.8 %reduce-scatter.18.cloned.1.call-start = ((), (), s32[]{:S(2)}) async-start(), calls=%async_computation.15 | async-start | bytes 11796480 | tf_op jit(solution)/shard_map/reduce_scatter | solution.py:265
  41.4 78.5 %copy-start.5 = (bf16[768,3,192]{2,1,0:T(4,128)(2,1)}, bf16[768,3,192]{2,1,0:T(4,128)(2,1)S(1)}, u32[]{:S(2)}) copy-start(bf16[768,3,192]{2,1,0:T(4,128)(2,1)S(1)} %all_gather.37) | copy-start | bytes 2654212
  61.4 61.5 %copy-start.13 = (f32[1024,8]{0,1:T(8,128)}, f32[1024,8]{0,1:T(8,128)S(1)}, u32[]{:S(2)}) copy-start(f32[1024,8]{0,1:T(8,128)S(1)} %get-tuple-element.171) | copy-start | bytes 98308
  296.2 99.6 %copy-start.7 = (bf16[3,1024,3,64]{1,3,2,0:T(8,128)(2,1)}, bf16[3,1024,3,64]{1,3,2,0:T(8,128)(2,1)S(1)}, u32[]{:S(2)}) copy-start(bf16[3,1024,3,64]{1,3,2,0:T(8,128)(2,1)S(1)} %pad_maximum_fusion.4) | copy-start | bytes 3538948
  296.4 99.5 %copy-start.8 = (bf16[3,1024,3,64]{1,3,2,0:T(8,128)(2,1)}, bf16[3,1024,3,64]{1,3,2,0:T(8,128)(2,1)S(1)}, u32[]{:S(2)}) copy-start(bf16[3,1024,3,64]{1,3,2,0:T(8,128)(2,1)S(1)} %pad_maximum_fusion.3) | copy-start | bytes 3538948
  303.0 369.2 %reduce-scatter.20.cloned.1.call-start = ((), (), s32[]{:S(2)}) async-start(), calls=%async_computation.16 | async-start | bytes 11796480 | tf_op jit(solution)/shard_map/reduce_scatter | solution.py:266
  363.0 473.7 %reduce-scatter.16.cloned.1.call-start = ((), (), s32[]{:S(2)}) async-start(), calls=%async_computation.13 | async-start | bytes 11796480 | tf_op jit(solution)/shard_map/reduce_scatter | solution.py:194
  395.8 499.8 %reduce-scatter.28.cloned.1.call-start = ((), (), s32[]{:S(2)}) async-start(), calls=%async_computation.20 | async-start | bytes 442368
  398.9 273.3 %copy-start.1 = (bf16[3,256,768]{2,1,0:T(8,128)(2,1)S(1)}, bf16[3,256,768]{2,1,0:T(8,128)(2,1)}, u32[]{:S(2)}) copy-start(bf16[3,256,768]{2,1,0:T(8,128)(2,1)} %param.13) | copy-start | bytes 3538948
  398.9 273.3 %copy-start.17 = (f32[3,256]{1,0:T(4,128)S(1)}, f32[3,256]{1,0:T(4,128)}, u32[]{:S(2)}) copy-start(f32[3,256]{1,0:T(4,128)} %copy-done.16) | copy-start | bytes 9220
  398.9 273.3 %copy-start.19 = (f32[768]{0:T(1024)S(1)}, f32[768]{0:T(1024)}, u32[]{:S(2)}) copy-start(f32[768]{0:T(1024)} %copy-done.18) | copy-start | bytes 9220
  398.9 273.3 %copy-start.21 = (f32[768]{0:T(1024)S(1)}, f32[768]{0:T(1024)}, u32[]{:S(2)}) copy-start(f32[768]{0:T(1024)} %copy-done.20) | copy-start | bytes 9220
  398.9 273.3 %copy-start.23 = (f32[3,256]{1,0:T(4,128)S(1)}, f32[3,256]{1,0:T(4,128)}, u32[]{:S(2)}) copy-start(f32[3,256]{1,0:T(4,128)} %copy-done.22) | copy-start | bytes 9220
  398.9 513.6 %reduce-scatter.30.cloned.1.call-start = ((), (), s32[]{:S(2)}) async-start(), calls=%async_computation.21 | async-start | bytes 884736
  404.2 545.2 %reduce-scatter.32.cloned.1.call-start = ((), (), s32[]{:S(2)}) async-start(), calls=%async_computation.22 | async-start | bytes 442368
  507.7 329.0 %copy-start.4 = (f32[3,256,768]{2,1,0:T(8,128)S(1)}, f32[3,256,768]{2,1,0:T(8,128)}, u32[]{:S(2)}) copy-start(f32[3,256,768]{2,1,0:T(8,128)} %reduce-scatter.18.cloned.1.call-done) | copy-start | bytes 7077892
  843.0 152.7 %reduce-scatter.22.cloned.1.call-start = ((), (), s32[]{:S(2)}) async-start(), calls=%async_computation.17 | async-start | bytes 2654208 | tf_op jit(solution)/shard_map/reduce_scatter | solution.py:292
  852.0 190.5 %reduce-scatter.24.cloned.1.call-start = ((), (), s32[]{:S(2)}) async-start(), calls=%async_computation.18 | async-start | bytes 2654208 | tf_op jit(solution)/shard_map/reduce_scatter | solution.py:294
  861.2 227.6 %reduce-scatter.26.cloned.1.call-start = ((), (), s32[]{:S(2)}) async-start(), calls=%async_computation.19 | async-start | bytes 2654208 | tf_op jit(solution)/shard_map/reduce_scatter | solution.py:295
  (24 other events, 305.8 us)
Sparse Core Ops, SparseCore 0:
  25.3 89.6 all-gather.8
  116.6 87.8 all-gather.16
  206.4 22.5 all-gather.12
  230.4 89.4 all-gather.10
  321.6 22.5 all-gather.14
  346.3 161.2 reduce-scatter.17
  510.0 162.1 reduce-scatter.19
  674.5 162.1 reduce-scatter.15
  839.7 34.6 reduce-scatter.27
  877.5 34.9 reduce-scatter.29
  915.6 33.8 reduce-scatter.31
  953.2 42.4 reduce-scatter.21
  1000.0 42.4 reduce-scatter.23
  1046.3 42.4 reduce-scatter.25
where the time goes:
time: 1100 us
  waiting for transfers between devices  710 us (65%)
  matrix products  175 us (16%)
  blocking collectives  87.6 us (8%)
  other arithmetic  83.2 us (8%)
  local copies, waits for them, and re-layouts  22.8 us (2%)
  between operations  15.4 us (1%)
    reduce_scatter x1, waiting for transfers between devices, local(): lax.psum_scatter(second_branch_gradient, 'tensor', scatter_dimension=1, t...  165 us
    reduce_scatter x1, waiting for transfers between devices, local(): lax.psum_scatter(partial_value, 'tensor', scatter_dimension=1, tiled=True)  156 us
    reduce_scatter x1, waiting for transfers between devices, local(): lax.psum_scatter(grad_first, 'tensor', scatter_dimension=1, tiled=True)  103 us
    unnamed x17, waiting for transfers between devices  53.9 us
    all_gather x1, waiting for transfers between devices, local(): lax.all_gather(first_low, 'tensor', axis=1, tiled=True)  53.7 us
    reduce_scatter x1, waiting for transfers between devices, local(): lax.psum_scatter(up_weight_gradient, 'dp', scatter_dimension=0, tiled=True)  46.8 us
    reduce_scatter x1, waiting for transfers between devices, local(): lax.psum_scatter(down_weight_gradient, 'dp', scatter_dimension=1, tiled=T...  46.3 us
    all_gather x1, waiting for transfers between devices, local(): incoming_gradient = lax.all_gather(cotangent, 'tensor', axis=1, tiled=True)  34.9 us
  transfers between devices with their start and end apart: 14, of which 12 were waited for; matrix products, arithmetic and copies ran while one was open for 25% of the time, Pallas kernels for 0%

commit v1 on v0

v1 whole, which is shorter than its diff:
```python
import functools

import jax
import jax.numpy as jnp
from jax import lax
from jax.experimental import pallas as pl
from jax.experimental.pallas import tpu as pltpu
from jax.sharding import PartitionSpec as P

HD = 64
ROT = 16
EPSILON = 1e-05
NEGATIVE = -1e30
TILE = 256
LANES = 128
F32 = jnp.float32
BF16 = jnp.bfloat16


def padded(width):
    return -(-width // LANES) * LANES


def rotary_tables(length, columns):
    half = ROT // 2
    positions = jnp.arange(length).astype(F32)
    frequency = 10000.0 ** (-jnp.arange(half).astype(F32) / half)
    angles = positions[:, None] * frequency[None, :]
    cosine, sine = jnp.cos(angles), jnp.sin(angles)
    zero = jnp.zeros_like(sine)
    rest = jnp.zeros((length, HD - ROT), F32)
    own = jnp.concatenate([cosine, cosine, rest + 1.0], 1)
    later = jnp.concatenate([-sine, zero, rest], 1)
    earlier = jnp.concatenate([zero, sine, rest], 1)
    return jnp.stack([jnp.tile(t, (1, columns // HD)) for t in (own, later, earlier)])


def dot(a, b, left, right):
    return lax.dot_general(a, b, (((left,), (right,)), ((), ())), preferred_element_type=F32)


def layer_kernel(first_call, heads, hid, *refs):
    if first_call:
        xg, w, vec, bu, bq, tab, both, gw, gs = refs[:9]
        refs = refs[9:]
        gw[...] = jnp.zeros_like(gw)
        gs[...] = jnp.zeros_like(gs)
    else:
        xg, w, vec, bu, bq, tab, gw_in, gs_in, both, gw, gs = refs[:11]
        refs = refs[11:]
        gw[...] = gw_in[...]
        gs[...] = gs_in[...]
    nrm, fst, outp, sp, q, k, v, do, att, dq, dk, dv = refs
    length, width = xg.shape[1], xg.shape[2]
    local = heads * HD
    pair = 2 * local
    up = slice(0, hid)
    down = slice(hid, 2 * hid)
    qkv_at = slice(2 * hid, 2 * hid + 3 * local)
    out_start = 2 * hid + padded(3 * local)
    out_at = slice(out_start, out_start + local)
    scale = HD ** (-0.5)

    def tables(rows):
        reps = pair // LANES
        return [jnp.concatenate([tab[n, rows, :]] * reps, axis=1) for n in range(3)]

    def before(i, carry):
        rows = pl.ds(pl.multiple_of(i * TILE, TILE), TILE)
        x = xg[0, rows, :].astype(F32)
        g = xg[1, rows, :]
        centre = x - jnp.mean(x, -1, keepdims=True)
        rsigma = lax.rsqrt(jnp.mean(centre * centre, -1, keepdims=True) + EPSILON)
        normed = centre * rsigma
        nrm[rows, :] = normed
        first = (normed * vec[0:1, :] + vec[1:2, :]).astype(BF16)
        second = (normed * vec[2:3, :] + vec[3:4, :]).astype(BF16)
        fst[rows, :] = first
        projected = dot(first, w[:, qkv_at], 1, 0) + bq[...]
        qk = projected[:, :pair]
        own, later, earlier = tables(rows)
        qk = qk * own + pltpu.roll(qk, pair - ROT // 2, 1) * later + pltpu.roll(qk, ROT // 2, 1) * earlier
        grad_att = dot(g, w[:, out_at], 1, 0)
        for h in range(heads):
            q[h, rows, :] = (qk[:, h * HD : (h + 1) * HD].astype(BF16).astype(F32) * scale).astype(BF16)
            k[h, rows, :] = qk[:, local + h * HD : local + (h + 1) * HD].astype(BF16)
            v[h, rows, :] = projected[:, pair + h * HD : pair + (h + 1) * HD].astype(BF16)
            do[h, rows, :] = grad_att[:, h * HD : (h + 1) * HD].astype(BF16)
        hidden = dot(second, w[:, up], 1, 0) + bu[...]
        cumulative = 0.5 * (1.0 + lax.erf(hidden * 0.7071067811865476))
        slope = cumulative + hidden * (jnp.exp(-0.5 * hidden * hidden) * 0.3989422804014327)
        act = (hidden * cumulative).astype(BF16)
        grad_pre32 = dot(g, w[:, down], 1, 0) * slope
        grad_pre = grad_pre32.astype(BF16)
        outp[rows, :] = dot(act, w[:, down], 1, 1)
        gw[:, down] += dot(g, act, 0, 0)
        gw[:, up] += dot(second, grad_pre, 0, 0)
        grad_second = dot(grad_pre, w[:, up], 1, 1)
        sp[rows, :] = grad_second * vec[2:3, :]
        gs[2:3, :width] += jnp.sum(grad_second * normed, 0, keepdims=True)
        gs[3:4, :width] += jnp.sum(grad_second, 0, keepdims=True)
        gs[4:5, :hid] += jnp.sum(grad_pre.astype(F32), 0, keepdims=True)
        return carry

    lax.fori_loop(0, length // TILE, before, 0)

    def head(h, carry):
        dk[h] = jnp.zeros((length, HD), F32)
        dv[h] = jnp.zeros((length, HD), F32)
        for i in range(length // TILE):
            rows = slice(i * TILE, (i + 1) * TILE)
            n = (i + 1) * TILE
            qi, doi = q[h, rows, :], do[h, rows, :]
            keys, values = k[h, :n, :], v[h, :n, :]
            scores = dot(qi, keys, 1, 1)
            column = lax.broadcasted_iota(jnp.int32, (TILE, n), 1)
            row = lax.broadcasted_iota(jnp.int32, (TILE, n), 0) + i * TILE
            scores = jnp.where(column <= row, scores, NEGATIVE)
            e = jnp.exp(scores - jnp.max(scores, -1, keepdims=True))
            probs = e * (1.0 / jnp.sum(e, -1, keepdims=True))
            low = probs.astype(BF16)
            att[h, rows, :] = dot(low, values, 1, 0).astype(BF16)
            grad_probs = dot(doi, values, 1, 1)
            inner = jnp.sum(probs * grad_probs, -1, keepdims=True)
            grad_scores = (probs * (grad_probs - inner)).astype(BF16)
            dq[h, rows, :] = dot(grad_scores, keys, 1, 0) * scale
            dk[h, :n, :] += dot(grad_scores, qi, 0, 0)
            dv[h, :n, :] += dot(low, doi, 0, 0)
        return carry

    lax.fori_loop(0, heads, head, 0)

    def after(i, carry):
        rows = pl.ds(pl.multiple_of(i * TILE, TILE), TILE)
        qk = jnp.concatenate([r[h, rows, :] for r in (dq, dk) for h in range(heads)], axis=1)
        own, later, earlier = tables(rows)
        qk = qk * own - pltpu.roll(qk, pair - ROT // 2, 1) * later - pltpu.roll(qk, ROT // 2, 1) * earlier
        grad = jnp.concatenate([qk] + [dv[h, rows, :] for h in range(heads)], axis=1).astype(BF16)
        attended = jnp.concatenate([att[h, rows, :].astype(F32) for h in range(heads)], axis=1).astype(BF16)
        g = xg[1, rows, :]
        normed = nrm[rows, :]
        gs[5:6, : 3 * local] += jnp.sum(grad.astype(F32), 0, keepdims=True)
        gw[:, qkv_at] += dot(fst[rows, :], grad, 0, 0)
        gw[:, out_at] += dot(g, attended, 0, 0)
        grad_first = dot(grad, w[:, qkv_at], 1, 1)
        gs[0:1, :width] += jnp.sum(grad_first * normed, 0, keepdims=True)
        gs[1:2, :width] += jnp.sum(grad_first, 0, keepdims=True)
        both[0, rows, :] = (outp[rows, :] + dot(attended, w[:, out_at], 1, 1)).astype(BF16)
        both[1, rows, :] = (sp[rows, :] + grad_first * vec[0:1, :]).astype(BF16)
        return carry

    lax.fori_loop(0, length // TILE, after, 0)


def layer(xg, w, vec, bu, bq, tab, sums):
    length, width = xg.shape[1], xg.shape[2]
    hid = bu.shape[1]
    local = bq.shape[1] // 3
    heads = local // HD
    most = max(width, hid, padded(3 * local))
    operands = (xg, w, vec, bu, bq, tab) + (() if sums is None else tuple(sums))
    whole = pl.BlockSpec(memory_space=pltpu.VMEM)
    perhead = (heads, length, HD)
    macs = length * width * (4 * local + 2 * hid) * 3 + 4 * heads * length * length * HD
    return pl.pallas_call(
        functools.partial(layer_kernel, sums is None, heads, hid),
        out_shape=(
            jax.ShapeDtypeStruct((2, length, width), BF16),
            jax.ShapeDtypeStruct(w.shape, F32),
            jax.ShapeDtypeStruct((8, most), F32),
        ),
        in_specs=[whole] * len(operands),
        out_specs=(whole,) * 3,
        scratch_shapes=[
            pltpu.VMEM((length, width), F32),
            pltpu.VMEM((length, width), BF16),
            pltpu.VMEM((length, width), F32),
            pltpu.VMEM((length, width), F32),
        ]
        + [pltpu.VMEM(perhead, BF16)] * 5
        + [pltpu.VMEM(perhead, F32)] * 3,
        compiler_params=pltpu.CompilerParams(vmem_limit_bytes=60 * 1024 * 1024),
        cost_estimate=pl.CostEstimate(
            flops=2 * macs, bytes_accessed=24 * 1024 * 1024, transcendentals=2 * length * hid + heads * length * length
        ),
    )(*operands)


def local(inputs, cotangent, w_qkv, b_qkv, w_attn_out, w_up, b_up, w_down, vectors):
    tensor_pos, tensor = lax.axis_index("tensor"), lax.axis_size("tensor")
    dp_pos, dp = lax.axis_index("dp"), lax.axis_size("dp")
    sequences, _, width = inputs.shape
    share, _, lw = w_qkv.shape
    hid = w_up.shape[1]
    folds = b_up.shape[0] // share
    qkv_pad = padded(3 * lw) - 3 * lw
    out_pad = padded(lw) - lw
    small = jnp.concatenate([b_qkv, vectors, b_up.reshape(folds, share)], 0).T
    packed = jnp.concatenate(
        [
            w_up,
            w_down.T,
            w_qkv.reshape(share, 3 * lw),
            jnp.pad(small, ((0, 0), (0, qkv_pad - small.shape[1]))),
            w_attn_out.T,
            jnp.zeros((share, out_pad), BF16),
        ],
        1,
    )
    w = lax.all_gather(packed, "dp", axis=0, tiled=True)
    pairs = [
        lax.all_gather(jnp.stack([inputs[s], cotangent[s]]), "tensor", axis=1, tiled=True) for s in range(sequences)
    ]
    length = pairs[0].shape[1]
    start = 2 * hid + 3 * lw
    rows = w[:, start : start + small.shape[1]].astype(F32).T
    vector_rows = rows[3:8]
    bq = lax.dynamic_slice_in_dim(rows[:3], tensor_pos * lw, lw, 1).reshape(1, 3 * lw)
    bias_up = rows[8:].reshape(folds, dp, share).transpose(1, 0, 2).reshape(-1)
    bu = lax.dynamic_slice_in_dim(bias_up, tensor_pos * hid, hid, 0).reshape(1, hid)
    vec = jnp.concatenate([vector_rows[:4], jnp.zeros((4, width), F32)], 0)
    tab = rotary_tables(length, LANES)

    sums, scattered = None, []
    for s in range(sequences):
        both, *sums = layer(pairs[s], w, vec, bu, bq, tab, sums)
        scattered.append(lax.psum_scatter(both, "tensor", scatter_dimension=1, tiled=True))
    gw, gs = sums

    cot = cotangent.astype(F32)
    grad_bq = lax.dynamic_update_slice_in_dim(
        jnp.zeros((3, width), F32), gs[5, : 3 * lw].reshape(3, lw), tensor_pos * lw, 1
    )
    grad_bu = lax.dynamic_update_slice_in_dim(jnp.zeros((hid * tensor,), F32), gs[4, :hid], tensor_pos * hid, 0)
    grad_bu = grad_bu.reshape(dp, folds, share).transpose(1, 0, 2).reshape(folds, width)
    little = jnp.concatenate([grad_bq, gs[:4, :width], jnp.sum(cot, axis=(0, 1))[None], grad_bu], 0)
    little = lax.psum(little, ("dp", "tensor"))
    little = lax.dynamic_slice_in_dim(little, dp_pos * share, share, 1)
    shares = lax.psum_scatter(gw.astype(BF16), "dp", scatter_dimension=0, tiled=True).astype(F32)

    outputs, grads = [], []
    for s in range(sequences):
        x = inputs[s].astype(F32)
        centre = x - jnp.mean(x, -1, keepdims=True)
        rsigma = lax.rsqrt(jnp.mean(centre * centre, -1, keepdims=True) + EPSILON)
        normed = centre * rsigma
        out_sum, back = scattered[s][0].astype(F32), scattered[s][1].astype(F32)
        outputs.append((x + out_sum + vector_rows[4]).astype(BF16))
        through = rsigma * (
            back - jnp.mean(back, -1, keepdims=True) - normed * jnp.mean(back * normed, -1, keepdims=True)
        )
        grads.append((cot[s] + through).astype(BF16))
    out_start = 2 * hid + padded(3 * lw)
    return (
        jnp.stack(outputs),
        jnp.stack(grads),
        shares[:, 2 * hid : start].reshape(share, 3, lw),
        little[:3],
        shares[:, out_start : out_start + lw].T,
        shares[:, :hid],
        little[8:].reshape(-1),
        shares[:, hid : 2 * hid].T,
        little[3:8],
    )


def solution(mesh):
    placed = (
        P("dp", "tensor", None),
        P("dp", "tensor", None),
        P("dp", None, "tensor"),
        P(None, "dp"),
        P("tensor", "dp"),
        P("dp", "tensor"),
        P("dp"),
        P("tensor", "dp"),
        P(None, "dp"),
    )
    return jax.shard_map(
        local,
        mesh=mesh,
        in_specs=placed,
        out_specs=placed,
        check_vma=False,
    )
```

time: 1100 us -> 542 us (0.49)
  waiting for transfers between devices: 710 us -> 325 us
  matrix products: 175 us -> 0 us
  Pallas kernels: 0 us -> 117 us
  other arithmetic: 83.2 us -> 26.4 us
  blocking collectives: 87.6 us -> 39.3 us
    reduce_scatter x6 -> x4, waiting for transfers between devices: 550 us -> 180 us  [the longest x3 179 us: local(): lax.psum_scatter(both, 'tensor', scatter_dimension=1, tiled=True)]
    dot_general x33 -> x0, matrix products: 175 us -> none  [the longest x3 24.6 us: attend_back(): jnp.einsum('qhe,khe->hqk', incoming_gradient, values_in, preferred_elemen...]
    pallas_call x0 -> x3, Pallas kernels: none -> 117 us  [layer(): pl.pallas_call(functools.partial(layer_kernel, sums is None, heads, hid),...]
    unnamed x17 -> x8, waiting for transfers between devices: 53.9 us -> 1.98 us
    all_gather x5 -> x0, blocking collectives: 51.6 us -> none  [the longest x1 13.2 us: local(): lax.all_gather(w_qkv, 'dp', axis=0, tiled=True)]
    convert_element_type x9 -> x6, other arithmetic: 47.9 us -> 9.37 us  [the longest x1 5.3 us: local(): gw.astype(BF16)]
    all_gather x5 -> x4, waiting for transfers between devices: 106 us -> 143 us  [the longest x3 113 us: local(): lax.all_gather(jnp.stack([inputs[s], cotangent[s]]), 'tensor', axis=1, ti...]
    psum x1, blocking collectives: 12.4 us -> 39.3 us  [local(): little = lax.psum(little, ('dp', 'tensor'))]
  transfers between devices with their start and end apart: 14 -> 8, of which waited for: 12 -> 8; matrix products, arithmetic and copies ran while one was open for 25% -> 5% of each run, Pallas kernels for 0% -> 14%
where the time goes in v1:
time: 542 us; the launch traced here: 541 us
  waiting for transfers between devices  325 us (60%)
  Pallas kernels  117 us (22%)
  blocking collectives  39.3 us (7%)
  other arithmetic  26.4 us (5%)
  local copies, waits for them, and re-layouts  18.3 us (3%)
  between operations  14.6 us (3%)
    reduce_scatter x3, waiting for transfers between devices, local(): lax.psum_scatter(both, 'tensor', scatter_dimension=1, tiled=True)  179 us
    pallas_call x3, Pallas kernels, layer(): pl.pallas_call(functools.partial(layer_kernel, sums is None, heads, hid),...  117 us
    all_gather x3, waiting for transfers between devices, local(): lax.all_gather(jnp.stack([inputs[s], cotangent[s]]), 'tensor', axis=1, ti...  113 us
    psum x1, blocking collectives, local(): little = lax.psum(little, ('dp', 'tensor'))  39.3 us
    all_gather x1, waiting for transfers between devices, local(): w = lax.all_gather(packed, 'dp', axis=0, tiled=True)  30.5 us
  transfers between devices with their start and end apart: 8, of which 8 were waited for; matrix products, arithmetic and copies ran while one was open for 5% of the time, Pallas kernels for 14%

profile of v1, /device:TPU:0, one launch (start us, length us, event | category | flops | bytes accessed | tf_op | source)
XLA Modules:
  0.0 541.3 jit_solution(15183913810723444831)
XLA Ops:
  7.2 1.2 copy.68
  11.1 1.9 concatenate.22
  13.0 1.4 fusion.43
  18.8 1.3 pad_maximum_fusion.refs_5_
  20.1 30.5 %all-gather.7.cloned.1.call-done.refs_1_ = bf16[768,2432]{1,0:T(8,128)(2,1)} async-done(((bf16[96,2432]{1,0:T(8,128)(2,1)}), bf16[768,2432]{1,0:T(8,128)(2,1)}) %all-gather.7.cloned.1.call-update) | async-done | bytes 3735568 | tf_op jit(solution)/shard_map/all_gather | solution.py:210
  54.0 62.2 %all-gather.5.cloned.1.call-done.refs_0_ = bf16[2,1024,768]{2,1,0:T(8,128)(2,1)} async-done(((bf16[2,256,768]{2,1,0:T(8,128)(2,1)}), bf16[2,1024,768]{2,1,0:T(8,128)(2,1)}) %all-gather.5.cloned.1.call-update) | async-done | bytes 3145744 | tf_op jit(solution)/shard_map/all_gather | solution.py:212
  116.2 37.6 %shard_map.160 = (bf16[2,1024,768]{2,1,0:T(8,128)(2,1)}, f32[768,2432]{1,0:T(8,128)}, f32[8,768]{1,0:T(8,128)}) custom-call(bf16[2,1024,768]{2,1,0:T(8,128)(2,1)} %all-gather.5.cloned.1.call-done.refs_0_, bf16[768,2432]{1,0:T(8,128)(2,1)} %all-gather.7.cloned.1.call-done.refs_1_, f32[8,768]{1,0:T(8,128)} %concatenate.23.refs_2_, f32[1,768]{1,0:T(1,128)} %reshape.270.refs_3_, ...), custom_call_target="tpu_custom_call" | custom-call | flops 12482248704 | bytes 25165824 | tf_op jit(solution)/shard_map/pallas_call | solution.py:165
  153.9 26.7 %all-gather.9.cloned.1.call-done.refs_0_ = bf16[2,1024,768]{2,1,0:T(8,128)(2,1)} async-done(((bf16[2,256,768]{2,1,0:T(8,128)(2,1)}), bf16[2,1024,768]{2,1,0:T(8,128)(2,1)}) %all-gather.9.cloned.1.call-update) | async-done | bytes 3145744 | tf_op jit(solution)/shard_map/all_gather | solution.py:212
  180.6 39.9 %shard_map.161 = (bf16[2,1024,768]{2,1,0:T(8,128)(2,1)}, f32[768,2432]{1,0:T(8,128)}, f32[8,768]{1,0:T(8,128)}) custom-call(bf16[2,1024,768]{2,1,0:T(8,128)(2,1)} %all-gather.9.cloned.1.call-done.refs_0_, bf16[768,2432]{1,0:T(8,128)(2,1)} %all-gather.7.cloned.1.call-done.refs_1_, f32[8,768]{1,0:T(8,128)} %concatenate.23.refs_2_, f32[1,768]{1,0:T(1,128)} %reshape.270.refs_3_, ...), custom_call_target="tpu_custom_call" | custom-call | flops 12482248704 | bytes 25165824 | tf_op jit(solution)/shard_map/pallas_call | solution.py:165
  220.4 23.7 %all-gather.11.cloned.1.call-done.refs_0_ = bf16[2,1024,768]{2,1,0:T(8,128)(2,1)} async-done(((bf16[2,256,768]{2,1,0:T(8,128)(2,1)}), bf16[2,1024,768]{2,1,0:T(8,128)(2,1)}) %all-gather.11.cloned.1.call-update) | async-done | bytes 3145744 | tf_op jit(solution)/shard_map/all_gather | solution.py:212
  244.2 39.9 %shard_map.162 = (bf16[2,1024,768]{2,1,0:T(8,128)(2,1)}, f32[768,2432]{1,0:T(8,128)}, f32[8,768]{1,0:T(8,128)}) custom-call(bf16[2,1024,768]{2,1,0:T(8,128)(2,1)} %all-gather.11.cloned.1.call-done.refs_0_, bf16[768,2432]{1,0:T(8,128)(2,1)} %all-gather.7.cloned.1.call-done.refs_1_, f32[8,768]{1,0:T(8,128)} %concatenate.23.refs_2_, ...), custom_call_target="tpu_custom_call" | custom-call | flops 12482248704 | bytes 25165824 | tf_op jit(solution)/shard_map/pallas_call | solution.py:165
  284.1 5.3 convert_element_type.143
  292.1 1.6 convert_element_type.130
  295.3 39.3 %psum.7 = f32[12,768]{1,0:T(8,128)S(1)} all-reduce(f32[12,768]{1,0:T(8,128)S(1)} %pad_maximum_fusion.6), channel_id=1, replica_groups=mesh['dp'=8,'tensor'=4] {'dp','tensor'}, use_global_device_ids=true, to_apply=%region_17.18 | all-reduce | flops 9216 | bytes 73728 | tf_op jit(solution)/shard_map/psum | solution.py:237
  336.7 1.2 reduce-scatter.11.cloned.1.call-done
  342.2 58.1 %reduce-scatter.5.cloned.1.call-done = bf16[2,256,768]{2,1,0:T(8,128)(2,1)} async-done(((bf16[2,1024,768]{2,1,0:T(8,128)(2,1)}), bf16[2,256,768]{2,1,0:T(8,128)(2,1)}) %reduce-scatter.5.cloned.1.call-update) | async-done | bytes 786448 | tf_op jit(solution)/shard_map/reduce_scatter | solution.py:227
  401.5 1.6 fusion.5
  405.3 57.7 %reduce-scatter.7.cloned.1.call-done = bf16[2,256,768]{2,1,0:T(8,128)(2,1)} async-done(((bf16[2,1024,768]{2,1,0:T(8,128)(2,1)}), bf16[2,256,768]{2,1,0:T(8,128)(2,1)}) %reduce-scatter.7.cloned.1.call-update) | async-done | bytes 786448 | tf_op jit(solution)/shard_map/reduce_scatter | solution.py:227
  463.0 62.7 %reduce-scatter.9.cloned.1.call-done = bf16[2,256,768]{2,1,0:T(8,128)(2,1)} async-done(((bf16[2,1024,768]{2,1,0:T(8,128)(2,1)}), bf16[2,256,768]{2,1,0:T(8,128)(2,1)}) %reduce-scatter.9.cloned.1.call-update) | async-done | bytes 786448 | tf_op jit(solution)/shard_map/reduce_scatter | solution.py:227
  525.8 1.6 fusion.11
  527.4 1.1 convert_reduce_fusion.3
  529.8 1.6 fusion.9
  532.2 1.1 pad_maximum_fusion.1
  533.4 1.1 pad_maximum_fusion.2
  (121 shorter events, 26.3 us)
Async XLA Ops:
  7.2 5.8 %copy-start = (bf16[3,256,768]{2,1,0:T(8,128)(2,1)S(1)}, bf16[3,256,768]{2,1,0:T(8,128)(2,1)}, u32[]{:S(2)}) copy-start(bf16[3,256,768]{2,1,0:T(8,128)(2,1)} %param.9) | copy-start | bytes 3538948
  7.2 43.4 %all-gather.7.cloned.1.call-start = ((), (), s32[]{:S(2)}) async-start(), calls=%async_computation.5 | async-start | bytes 4202496 | tf_op jit(solution)/shard_map/all_gather | solution.py:210
  13.0 103.3 %all-gather.5.cloned.1.call-start = ((), (), s32[]{:S(2)}) async-start(), calls=%async_computation.4 | async-start | bytes 3932160 | tf_op jit(solution)/shard_map/all_gather | solution.py:212
  15.4 165.2 %all-gather.9.cloned.1.call-start = ((), (), s32[]{:S(2)}) async-start(), calls=%async_computation.7 | async-start | bytes 3932160 | tf_op jit(solution)/shard_map/all_gather | solution.py:212
  16.4 227.8 %all-gather.11.cloned.1.call-start = ((), (), s32[]{:S(2)}) async-start(), calls=%async_computation.9 | async-start | bytes 3932160 | tf_op jit(solution)/shard_map/all_gather | solution.py:212
  17.5 320.4 %reduce-scatter.11.cloned.1.call-start = ((), (), s32[]{:S(2)}) async-start(), calls=%async_computation.11 | async-start | bytes 4202496 | tf_op jit(solution)/shard_map/reduce_scatter | solution.py:239
  289.4 110.9 %reduce-scatter.5.cloned.1.call-start = ((), (), s32[]{:S(2)}) async-start(), calls=%async_computation.6 | async-start | bytes 3932160 | tf_op jit(solution)/shard_map/reduce_scatter | solution.py:227
  290.0 173.0 %reduce-scatter.7.cloned.1.call-start = ((), (), s32[]{:S(2)}) async-start(), calls=%async_computation.8 | async-start | bytes 3932160 | tf_op jit(solution)/shard_map/reduce_scatter | solution.py:227
  290.8 235.0 %reduce-scatter.9.cloned.1.call-start = ((), (), s32[]{:S(2)}) async-start(), calls=%async_computation.10 | async-start | bytes 3932160 | tf_op jit(solution)/shard_map/reduce_scatter | solution.py:227
  290.8 1.3 copy-start.1
  293.7 0.8 copy-start.6
  294.4 107.0 %copy-start.8 = (f32[256]{0:T(256)}, f32[256]{0:T(256)S(1)}, u32[]{:S(2)}) copy-start(f32[256]{0:T(256)S(1)} %add_rsqrt_fusion.2) | copy-start | bytes 3076
  337.9 2.0 copy-start.5
  405.3 124.4 %copy-start.2 = (f32[3,256,768]{2,1,0:T(8,128)S(1)}, f32[3,256,768]{2,1,0:T(8,128)}, u32[]{:S(2)}) copy-start(f32[3,256,768]{2,1,0:T(8,128)} %convert_element_type.130) | copy-start | bytes 7077892
  529.7 1.7 copy-start.3
  529.7 1.7 copy-start.4
  529.7 1.7 copy-start.7
  529.7 1.7 copy-start.9
  529.7 1.7 copy-start.10
  529.8 1.7 copy-start.11
Sparse Core Ops, SparseCore 0:
  13.1 37.4 all-gather.6
  52.7 63.4 all-gather.4
  118.4 62.1 all-gather.8
  182.0 62.1 all-gather.10
  289.5 48.3 reduce-scatter.10
  340.2 60.1 reduce-scatter.4
  402.7 60.2 reduce-scatter.6
  465.4 60.2 reduce-scatter.8

commit v2 on v1

--- a/solution.py
+++ b/solution.py
@@ -39,7 +39,131 @@
     return lax.dot_general(a, b, (((left,), (right,)), ((), ())), preferred_element_type=F32)
 
 
-def layer_kernel(first_call, heads, hid, *refs):
+class Line:
+    def __init__(self, own, target, local_sem, send_sem, recv_sem, n):
+        self.own, self.target, self.n = own, target, n
+        self.local_sem, self.send_sem, self.recv_sem = local_sem, send_sem, recv_sem
+        self.me = lax.axis_index("tensor")
+
+    def slot(self, j):
+        block = self.own.shape[1]
+        return self.target.at[:, pl.ds(pl.multiple_of(j * block, block), block), :]
+
+    def sent(self, way, step):
+        me = self.me
+        j = me - (step - 1) if way == 0 else me + (step - 1)
+        moves = (me < self.n - 1) & (j >= 0) if way == 0 else (me > 0) & (j < self.n)
+        return moves, j, (me + 1 if way == 0 else me - 1)
+
+    def copy(self, way, step, j, other, first):
+        return pltpu.make_async_remote_copy(
+            src_ref=self.own if first else self.slot(j),
+            dst_ref=self.slot(j),
+            send_sem=self.send_sem.at[way, step - 1],
+            recv_sem=self.recv_sem.at[way, step - 1],
+            device_id={"tensor": other},
+            device_id_type=pl.DeviceIdType.MESH,
+        )
+
+    def launch(self, step):
+        for way in (0, 1):
+            moves, j, other = self.sent(way, step)
+
+            @pl.when(moves)
+            def _():
+                self.copy(way, step, j, other, step == 1).start()
+
+    def arrive(self, step):
+        for way in (0, 1):
+            j = self.me - step if way == 0 else self.me + step
+            other = self.me - 1 if way == 0 else self.me + 1
+
+            @pl.when(j >= 0 if way == 0 else j < self.n)
+            def _():
+                self.copy(way, step, j, other, False).wait_recv()
+
+    def begin(self):
+        me, barrier = self.me, pltpu.get_barrier_semaphore()
+        for there, other in ((me > 0, me - 1), (me < self.n - 1, me + 1)):
+
+            @pl.when(there)
+            def _():
+                pl.semaphore_signal(
+                    barrier, inc=1, device_id={"tensor": other}, device_id_type=pl.DeviceIdType.MESH
+                )
+
+        ends = (me == 0) | (me == self.n - 1)
+
+        @pl.when(ends)
+        def _():
+            pl.semaphore_wait(barrier, 1)
+
+        @pl.when(jnp.logical_not(ends))
+        def _():
+            pl.semaphore_wait(barrier, 2)
+
+        pltpu.make_async_copy(self.own, self.slot(me), self.local_sem).start()
+        self.launch(1)
+        self.step = 1
+
+    def advance(self):
+        if self.step < self.n - 1:
+            self.arrive(self.step)
+            self.step += 1
+            self.launch(self.step)
+
+    def finish(self):
+        while self.step < self.n - 1:
+            self.advance()
+        self.arrive(self.step)
+        for step in range(1, self.n):
+            for way in (0, 1):
+                moves, j, other = self.sent(way, step)
+
+                @pl.when(moves)
+                def _():
+                    self.copy(way, step, j, other, step == 1).wait_send()
+
+        pltpu.make_async_copy(self.own, self.slot(self.me), self.local_sem).wait()
+
+
+def line_scratch(n):
+    return [
+        pltpu.SemaphoreType.DMA,
+        pltpu.SemaphoreType.DMA((2, n - 1)),
+        pltpu.SemaphoreType.DMA((2, n - 1)),
+    ]
+
+
+def gather_kernel(n, own, target, *sems):
+    line = Line(own, target, *sems, n)
+    line.begin()
+    line.finish()
+
+
+def gather(own):
+    n = lax.axis_size("tensor")
+    return pl.pallas_call(
+        functools.partial(gather_kernel, n),
+        out_shape=jax.ShapeDtypeStruct((own.shape[0], own.shape[1] * n, own.shape[2]), own.dtype),
+        in_specs=[pl.BlockSpec(memory_space=pl.ANY)],
+        out_specs=pl.BlockSpec(memory_space=pl.ANY),
+        scratch_shapes=line_scratch(n),
+        compiler_params=pltpu.CompilerParams(collective_id=0, has_side_effects=True),
+        cost_estimate=pl.CostEstimate(flops=0, bytes_accessed=160 * 1024 * 1024, transcendentals=0),
+    )(own)
+
+
+def layer_kernel(first_call, heads, hid, n, waits, *refs):
+    refs = refs[waits:]
+    line = None
+    if n:
+        own_block, refs = refs[0], refs[1:]
+        at = 9 if first_call else 11
+        target, refs = refs[at], refs[:at] + refs[at + 1 :]
+        line = Line(own_block, target, *refs[-3:], n)
+        refs = refs[:-3]
+        line.begin()
     if first_call:
         xg, w, vec, bu, bq, tab, both, gw, gs = refs[:9]
         refs = refs[9:]
@@ -103,6 +227,8 @@
         return carry
 
     lax.fori_loop(0, length // TILE, before, 0)
+    if line:
+        line.advance()
 
     def head(h, carry):
         dk[h] = jnp.zeros((length, HD), F32)
@@ -129,6 +255,8 @@
         return carry
 
     lax.fori_loop(0, heads, head, 0)
+    if line:
+        line.advance()
 
     def after(i, carry):
         rows = pl.ds(pl.multiple_of(i * TILE, TILE), TILE)
@@ -150,9 +278,11 @@
         return carry
 
     lax.fori_loop(0, length // TILE, after, 0)
-
-
-def layer(xg, w, vec, bu, bq, tab, sums):
+    if line:
+        line.finish()
+
+
+def layer(xg, w, vec, bu, bq, tab, sums, own, call, waits):
     length, width = xg.shape[1], xg.shape[2]
     hid = bu.shape[1]
     local = bq.shape[1] // 3
@@ -160,17 +290,21 @@
     most = max(width, hid, padded(3 * local))
     operands = (xg, w, vec, bu, bq, tab) + (() if sums is None else tuple(sums))
     whole = pl.BlockSpec(memory_space=pltpu.VMEM)
+    anywhere = pl.BlockSpec(memory_space=pl.ANY)
+    n = 0 if own is None else lax.axis_size("tensor")
+    remote = dict(collective_id=call, has_side_effects=True) if n else {}
     perhead = (heads, length, HD)
     macs = length * width * (4 * local + 2 * hid) * 3 + 4 * heads * length * length * HD
     return pl.pallas_call(
-        functools.partial(layer_kernel, sums is None, heads, hid),
+        functools.partial(layer_kernel, sums is None, heads, hid, n, len(waits)),
         out_shape=(
             jax.ShapeDtypeStruct((2, length, width), BF16),
             jax.ShapeDtypeStruct(w.shape, F32),
             jax.ShapeDtypeStruct((8, most), F32),
-        ),
-        in_specs=[whole] * len(operands),
-        out_specs=(whole,) * 3,
+        )
+        + ((jax.ShapeDtypeStruct(xg.shape, BF16),) if n else ()),
+        in_specs=[anywhere] * (len(waits) + bool(n)) + [whole] * len(operands),
+        out_specs=(whole,) * 3 + ((anywhere,) if n else ()),
         scratch_shapes=[
             pltpu.VMEM((length, width), F32),
             pltpu.VMEM((length, width), BF16),
@@ -178,12 +312,13 @@
             pltpu.VMEM((length, width), F32),
         ]
         + [pltpu.VMEM(perhead, BF16)] * 5
-        + [pltpu.VMEM(perhead, F32)] * 3,
-        compiler_params=pltpu.CompilerParams(vmem_limit_bytes=60 * 1024 * 1024),
+        + [pltpu.VMEM(perhead, F32)] * 3
+        + (line_scratch(n) if n else []),
+        compiler_params=pltpu.CompilerParams(vmem_limit_bytes=60 * 1024 * 1024, **remote),
         cost_estimate=pl.CostEstimate(
             flops=2 * macs, bytes_accessed=24 * 1024 * 1024, transcendentals=2 * length * hid + heads * length * length
         ),
-    )(*operands)
+    )(*waits, *((own,) if n else ()), *operands)
 
 
 def local(inputs, cotangent, w_qkv, b_qkv, w_attn_out, w_up, b_up, w_down, vectors):
@@ -208,10 +343,9 @@
         1,
     )
     w = lax.all_gather(packed, "dp", axis=0, tiled=True)
-    pairs = [
-        lax.all_gather(jnp.stack([inputs[s], cotangent[s]]), "tensor", axis=1, tiled=True) for s in range(sequences)
-    ]
-    length = pairs[0].shape[1]
+    blocks = [jnp.stack([inputs[s], cotangent[s]]) for s in range(sequences)]
+    pair = gather(blocks[0])
+    length = pair.shape[1]
     start = 2 * hid + 3 * lw
     rows = w[:, start : start + small.shape[1]].astype(F32).T
     vector_rows = rows[3:8]
@@ -223,9 +357,10 @@
 
     sums, scattered = None, []
     for s in range(sequences):
-        both, *sums = layer(pairs[s], w, vec, bu, bq, tab, sums)
+        ahead = blocks[s + 1] if s + 1 < sequences else None
+        both, gw, gs, *pair = layer(pair, w, vec, bu, bq, tab, sums, ahead, s + 1, scattered[: max(s - 1, 0)][-1:])
+        sums, pair = (gw, gs), (pair[0] if pair else None)
         scattered.append(lax.psum_scatter(both, "tensor", scatter_dimension=1, tiled=True))
-    gw, gs = sums
 
     cot = cotangent.astype(F32)
     grad_bq = lax.dynamic_update_slice_in_dim(
@@ -236,6 +371,8 @@
     little = jnp.concatenate([grad_bq, gs[:4, :width], jnp.sum(cot, axis=(0, 1))[None], grad_bu], 0)
     little = lax.psum(little, ("dp", "tensor"))
     little = lax.dynamic_slice_in_dim(little, dp_pos * share, share, 1)
+    if sequences > 1:
+        gw, scattered[-2] = lax.optimization_barrier((gw, scattered[-2]))
     shares = lax.psum_scatter(gw.astype(BF16), "dp", scatter_dimension=0, tiled=True).astype(F32)
 
     outputs, grads = [], []

time: 542 us -> 447 us (0.82)
  waiting for transfers between devices: 325 us -> 73.7 us
  Pallas kernels: 117 us -> 270 us
    pallas_call x3 -> x4, Pallas kernels: 117 us -> 270 us  [the longest x3 212 us: layer(): pl.pallas_call(functools.partial(layer_kernel, sums is None, heads, hid,...]
    all_gather x3 -> x0, waiting for transfers between devices: 113 us -> none  [local(): lax.all_gather(jnp.stack([inputs[s], cotangent[s]]), 'tensor', axis=1, ti...]
    reduce_scatter x3, waiting for transfers between devices: 179 us -> 73.1 us  [local(): lax.psum_scatter(both, 'tensor', scatter_dimension=1, tiled=True)]
    all_gather x1, waiting for transfers between devices: 30.5 us -> 0.01 us  [local(): w = lax.all_gather(packed, 'dp', axis=0, tiled=True)]
  transfers between devices with their start and end apart: 8 -> 5, of which waited for: 8 -> 2; matrix products, arithmetic and copies ran while one was open for 5% -> 5% of each run, Pallas kernels for 14% -> 47%
where the time goes in v2:
time: 447 us; the launch traced here: 446 us
  Pallas kernels  270 us (60%)
  waiting for transfers between devices  73.7 us (16%)
  blocking collectives  40.9 us (9%)
  other arithmetic  24.4 us (5%)
  local copies, waits for them, and re-layouts  22.8 us (5%)
  between operations  14.3 us (3%)
    pallas_call x3, Pallas kernels, layer(): pl.pallas_call(functools.partial(layer_kernel, sums is None, heads, hid,...  212 us
    reduce_scatter x3, waiting for transfers between devices, local(): lax.psum_scatter(both, 'tensor', scatter_dimension=1, tiled=True)  73.1 us
    pallas_call x1, Pallas kernels, gather(): pl.pallas_call(functools.partial(gather_kernel, n), out_shape=jax.ShapeDt...  57.7 us
    psum x1, blocking collectives, local(): little = lax.psum(little, ('dp', 'tensor'))  40.9 us
  transfers between devices with their start and end apart: 5, of which 2 were waited for; matrix products, arithmetic and copies ran while one was open for 5% of the time, Pallas kernels for 47%

profile of v2, /device:TPU:0, one launch (start us, length us, event | category | flops | bytes accessed | tf_op | source)
XLA Modules:
  0.0 446.3 jit_solution(3020105894362295902)
XLA Ops:
  9.7 1.1 copy.68
  11.0 1.9 concatenate.22
  14.0 1.0 copy.74
  17.7 1.3 pad_maximum_fusion.3
  18.9 57.7 %shard_map.160.refs_1_ = bf16[2,1024,768]{2,1,0:T(8,128)(2,1)} custom-call(bf16[2,256,768]{2,1,0:T(8,128)(2,1)} %get-tuple-element.110.own), custom_call_target="tpu_custom_call" | custom-call | bytes 167772160 | tf_op jit(solution)/shard_map/pallas_call | solution.py:146
  76.7 2.3 pad_maximum_fusion.refs_6_
  79.0 1.0 slice.128
  82.4 58.8 %shard_map.161 = (bf16[2,1024,768]{2,1,0:T(8,128)(2,1)}, f32[768,2432]{1,0:T(8,128)}, f32[8,768]{1,0:T(8,128)}, bf16[2,1024,768]{2,1,0:T(8,128)(2,1)}) custom-call(bf16[2,256,768]{2,1,0:T(8,128)(2,1)} %get-tuple-element.109.refs_0_, bf16[2,1024,768]{2,1,0:T(8,128)(2,1)} %shard_map.160.refs_1_, bf16[768,2432]{1,0:T(8,128)(2,1)} %all-gather.2.cloned.1.call-done.refs_2_, ...), custom_call_target="tpu_custom_call" | custom-call | flops 12482248704 | bytes 25165824 | tf_op jit(solution)/shard_map/pallas_call | solution.py:298
  142.3 0.9 pad_maximum_fusion.5.refs_0_
  143.2 112.9 %shard_map.162 = (bf16[2,1024,768]{2,1,0:T(8,128)(2,1)}, f32[768,2432]{1,0:T(8,128)}, f32[8,768]{1,0:T(8,128)}, bf16[2,1024,768]{2,1,0:T(8,128)(2,1)}) custom-call(bf16[2,256,768]{2,1,0:T(8,128)(2,1)} %pad_maximum_fusion.5.refs_0_, bf16[2,1024,768]{2,1,0:T(8,128)(2,1)} %get-tuple-element.23.refs_1_, bf16[768,2432]{1,0:T(8,128)(2,1)} %all-gather.2.cloned.1.call-done.refs_2_, ...), custom_call_target="tpu_custom_call" | custom-call | flops 12482248704 | bytes 25165824 | tf_op jit(solution)/shard_map/pallas_call | solution.py:298
  256.5 40.3 %shard_map.163 = (bf16[2,1024,768]{2,1,0:T(8,128)(2,1)}, f32[768,2432]{1,0:T(8,128)}, f32[8,768]{1,0:T(8,128)}) custom-call(bf16[2,256,768]{2,1,0:T(8,128)(2,1)} %reduce-scatter.5.cloned.1.call-done.refs_0_, bf16[2,1024,768]{2,1,0:T(8,128)(2,1)} %get-tuple-element.26.refs_1_, bf16[768,2432]{1,0:T(8,128)(2,1)} %all-gather.2.cloned.1.call-done.refs_2_, ...), custom_call_target="tpu_custom_call" | custom-call | flops 12482248704 | bytes 25165824 | tf_op jit(solution)/shard_map/pallas_call | solution.py:298
  296.7 18.0 %reduce-scatter.7.cloned.1.call-done = bf16[2,256,768]{2,1,0:T(8,128)(2,1)} async-done(((bf16[2,1024,768]{2,1,0:T(8,128)(2,1)}), bf16[2,256,768]{2,1,0:T(8,128)(2,1)}) %reduce-scatter.7.cloned.1.call-update) | async-done | bytes 786448 | tf_op jit(solution)/shard_map/reduce_scatter | solution.py:363
  314.8 5.3 %convert_element_type.143 = bf16[768,2432]{1,0:T(8,128)(2,1)} convert(f32[768,2432]{1,0:T(8,128)} %get-tuple-element.33) | non-fusion elementwise | flops 1867776 | bytes 11206656 | tf_op jit(solution)/shard_map/convert_element_type | solution.py:376
  320.7 1.6 convert_element_type.130
  324.0 40.9 %psum.7 = f32[12,768]{1,0:T(8,128)S(1)} all-reduce(f32[12,768]{1,0:T(8,128)S(1)} %pad_maximum_fusion.6), channel_id=1, replica_groups=mesh['dp'=8,'tensor'=4] {'dp','tensor'}, use_global_device_ids=true, to_apply=%region_17.18 | all-reduce | flops 9216 | bytes 73728 | tf_op jit(solution)/shard_map/psum | solution.py:372
  370.7 1.0 slice.140
  372.8 0.9 copy-done.8
  375.2 1.8 slice_bitcast_fusion
  377.1 55.1 %reduce-scatter.9.cloned.1.call-done = bf16[2,256,768]{2,1,0:T(8,128)(2,1)} async-done(((bf16[2,1024,768]{2,1,0:T(8,128)(2,1)}), bf16[2,256,768]{2,1,0:T(8,128)(2,1)}) %reduce-scatter.9.cloned.1.call-update) | async-done | bytes 786448 | tf_op jit(solution)/shard_map/reduce_scatter | solution.py:363
  432.2 1.1 convert_reduce_fusion.3
  433.3 1.6 fusion.11
  435.0 1.6 fusion.9
  437.5 1.1 pad_maximum_fusion.2
  438.6 1.1 pad_maximum_fusion.1
  (123 shorter events, 21.4 us)
Async XLA Ops:
  7.2 71.8 %all-gather.2.cloned.1.call-start = ((), (), s32[]{:S(2)}) async-start(), calls=%async_computation.4 | async-start | bytes 4202496 | tf_op jit(solution)/shard_map/all_gather | solution.py:345
  12.9 243.6 %reduce-scatter.5.cloned.1.call-start = ((), (), s32[]{:S(2)}) async-start(), calls=%async_computation.5 | async-start | bytes 3932160 | tf_op jit(solution)/shard_map/reduce_scatter | solution.py:363
  13.9 1.5 copy-start.1
  15.4 1.4 copy-start
  141.2 1.0 copy-start.9
  141.2 1.1 copy-start.10
  141.2 173.6 %reduce-scatter.7.cloned.1.call-start = ((), (), s32[]{:S(2)}) async-start(), calls=%async_computation.6 | async-start | bytes 3932160 | tf_op jit(solution)/shard_map/reduce_scatter | solution.py:363
  256.2 114.5 %reduce-scatter.11.cloned.1.call-start = ((), (), s32[]{:S(2)}) async-start(), calls=%async_computation.8 | async-start | bytes 4202496 | tf_op jit(solution)/shard_map/reduce_scatter | solution.py:376
  320.1 112.1 %reduce-scatter.9.cloned.1.call-start = ((), (), s32[]{:S(2)}) async-start(), calls=%async_computation.7 | async-start | bytes 3932160 | tf_op jit(solution)/shard_map/reduce_scatter | solution.py:363
  322.3 0.8 copy-start.11
  322.6 44.4 %copy-start.6 = (bf16[2,256,768]{2,1,0:T(8,128)(2,1)S(1)}, bf16[2,256,768]{2,1,0:T(8,128)(2,1)}, u32[]{:S(2)}) copy-start(bf16[2,256,768]{2,1,0:T(8,128)(2,1)} %reduce-scatter.7.cloned.1.call-done) | copy-start | bytes 2359300
  322.6 44.6 %copy-start.3 = (bf16[2,256,768]{2,1,0:T(8,128)(2,1)S(1)}, bf16[2,256,768]{2,1,0:T(8,128)(2,1)}, u32[]{:S(2)}) copy-start(bf16[2,256,768]{2,1,0:T(8,128)(2,1)} %reduce-scatter.5.cloned.1.call-done.refs_0_) | copy-start | bytes 2359300
  323.1 44.7 %copy-start.13 = (f32[256]{0:T(256)}, f32[256]{0:T(256)S(1)}, u32[]{:S(2)}) copy-start(f32[256]{0:T(256)S(1)} %add_rsqrt_fusion.2) | copy-start | bytes 3076
  370.7 2.0 copy-start.7
  372.8 0.9 copy-start.8
  375.2 59.7 %copy-start.2 = (f32[3,256,768]{2,1,0:T(8,128)S(1)}, f32[3,256,768]{2,1,0:T(8,128)}, u32[]{:S(2)}) copy-start(f32[3,256,768]{2,1,0:T(8,128)} %convert_element_type.130) | copy-start | bytes 7077892
  435.0 1.7 copy-start.4
  435.0 1.7 copy-start.5
  435.0 1.7 copy-start.12
  435.0 1.7 copy-start.14
  435.0 1.7 copy-start.15
  435.0 1.7 copy-start.16
Sparse Core Ops, SparseCore 0:
  13.0 37.4 all-gather.1
  141.3 81.2 reduce-scatter.4
  256.3 58.4 reduce-scatter.6
  320.2 49.4 reduce-scatter.10
  371.9 60.2 reduce-scatter.8
